TPU v7x, 256 devices: a whole 4x4x8 slice. The times are simulated.
256 devices in a mesh: cp: 64 (over y, z, core), hp: 4 (over x).
Axes of the slice: x: 4, y: 4, z: 8, core: 2. Of those that a mesh axis runs over, the one named last changes fastest.
Arguments:
- query: bfloat16 [32768, 4096], P(('cp', 'hp')), may hold values from -6 to 6
- key: bfloat16 [32768, 512], P(('cp', 'hp')), may hold values from -6 to 6
- value: bfloat16 [32768, 512], P(('cp', 'hp')), may hold values from -6 to 6
- cotangent: bfloat16 [32768, 4096], P(('cp', 'hp')), may hold values from -6 to 6
- lengths: int32 [64], replicated, may hold values from 1 to 1536, 32768 in all
Outputs:
- attended: bfloat16 [32768, 4096], P(('cp', 'hp'))
- grad_query: bfloat16 [32768, 4096], P(('cp', 'hp'))
- grad_key: bfloat16 [32768, 512], P(('cp', 'hp'))
- grad_value: bfloat16 [32768, 512], P(('cp', 'hp'))
Inputs may be any that keep to these rules, and one draw needn't show every extreme that they name: The lengths sum to 32768 and the largest is exactly 1536.
All inputs are finite; a program needn't handle non-finite values.
Results may differ from a plain program's by a relative error of at most 0.0087.
Values may be sent and summed in bfloat16 or wider, within the bound.
A program may use at most 128 MiB of HBM per device.

v0:
```python
import functools
import math

import jax
import jax.numpy as jnp
from jax import lax
from jax.experimental import pallas as pl
from jax.experimental.pallas import tpu as pltpu
from jax.sharding import PartitionSpec as P

HEAD = 128
REACH = 3
TILE = 256
TILES = 7
CHUNK_HEADS = 2
OUTSIDE = -16384.0
NT = (((1,), (1,)), ((), ()))
TN = (((0,), (0,)), ((), ()))
NN = (((1,), (0,)), ((), ()))
F32 = jnp.float32
BF16 = jnp.bfloat16
MESH = pl.DeviceIdType.MESH


def dot(a, b, dims):
    return lax.dot_general(a, b, dims, preferred_element_type=F32)


def kernel(
    cp_size, hp_size, tokens, heads,
    query, key, value, cotangent, lens,
    attended, grad_query, grad_key, grad_value,
    qb, db, kx, vx, qe, s0, s1, pb, dsb, ob, dqb, acc, inv, dox, qn, don, akk, avv, sendb, recvb, gb,
    kv_send, kv_recv, win_send, win_recv, q_send, q_recv, d_send, d_recv,
    o_send, o_recv, dq_send, dq_recv, part_send, part_recv, g_send, g_recv, local,
):
    shard = tokens * hp_size
    pairs = shard // TILE
    window = (REACH + 1) * shard
    chunks = heads // CHUNK_HEADS
    rows = TILE * CHUNK_HEADS
    wide = CHUNK_HEADS * HEAD
    group = heads * HEAD
    place = lax.axis_index("cp")
    me = lax.axis_index("hp")
    scale = HEAD ** -0.5
    to_log2 = scale * math.log2(math.e)
    others = range(1, hp_size)
    mine = pl.ds(pl.multiple_of(me * tokens, tokens), tokens)

    def hp_peer(step):
        return lax.rem(me + step, hp_size)

    def cp_peer(step):
        return lax.rem(place + step + cp_size, cp_size)

    barrier = pltpu.get_barrier_semaphore()
    for step in others:
        pl.semaphore_signal(barrier, 1, device_id=(place, hp_peer(step)), device_id_type=MESH)
    for step in range(1, REACH + 1):
        pl.semaphore_signal(barrier, 1, device_id=(cp_peer(step), me), device_id_type=MESH)
        pl.semaphore_signal(barrier, 1, device_id=(cp_peer(-step), me), device_id_type=MESH)
    pl.semaphore_wait(barrier, hp_size - 1 + 2 * REACH)

    def columns(start, width):
        return pl.ds(pl.multiple_of(start, HEAD), width)

    def kv_copy(which, step):
        source, landing = ((key, kx), (value, vx))[which]
        to = hp_peer(step)
        return pltpu.make_async_remote_copy(
            src_ref=source.at[:, columns(to * HEAD, HEAD)],
            dst_ref=landing.at[pl.ds(pl.multiple_of(REACH * shard + me * tokens, tokens), tokens), pl.ds(0, HEAD)],
            send_sem=kv_send.at[which, step - 1], recv_sem=kv_recv.at[which, step - 1],
            device_id=(place, to), device_id_type=MESH)

    def in_copy(which, chunk, step):
        source, landing, send, recv = ((query, qb, q_send, q_recv), (cotangent, db, d_send, d_recv))[which]
        to = hp_peer(step)
        return pltpu.make_async_remote_copy(
            src_ref=source.at[:, columns(to * group + chunk * wide, wide)],
            dst_ref=landing.at[mine, columns(chunk * wide, wide)],
            send_sem=send.at[chunk, step - 1], recv_sem=recv.at[chunk, step - 1],
            device_id=(place, to), device_id_type=MESH)

    def out_copy(which, chunk, step):
        source, landing, send, recv = ((ob, attended, o_send, o_recv), (dqb, grad_query, dq_send, dq_recv))[which]
        to = hp_peer(step)
        return pltpu.make_async_remote_copy(
            src_ref=source.at[pl.ds(pl.multiple_of(to * tokens, tokens), tokens), columns(chunk * wide, wide)],
            dst_ref=landing.at[:, columns(me * group + chunk * wide, wide)],
            send_sem=send.at[chunk, step - 1], recv_sem=recv.at[chunk, step - 1],
            device_id=(place, to), device_id_type=MESH)

    def window_copy(which, step):
        ref = (kx, vx)[which]
        return pltpu.make_async_remote_copy(
            src_ref=ref.at[pl.ds(REACH * shard, shard), pl.ds(0, HEAD)],
            dst_ref=ref.at[pl.ds((REACH - step) * shard, shard), pl.ds(0, HEAD)],
            send_sem=win_send.at[which, step - 1], recv_sem=win_recv.at[which, step - 1],
            device_id=(cp_peer(step), me), device_id_type=MESH)

    def part_copy(block):
        return pltpu.make_async_remote_copy(
            src_ref=sendb.at[block], dst_ref=recvb.at[block],
            send_sem=part_send.at[block], recv_sem=part_recv.at[block],
            device_id=(cp_peer(block - REACH), me), device_id_type=MESH)

    def grad_copy(which, step):
        to = hp_peer(step)
        return pltpu.make_async_remote_copy(
            src_ref=gb.at[which, pl.ds(pl.multiple_of(to * tokens, tokens), tokens), :],
            dst_ref=(grad_key, grad_value)[which].at[:, columns(me * HEAD, HEAD)],
            send_sem=g_send.at[which, step - 1], recv_sem=g_recv.at[which, step - 1],
            device_id=(place, to), device_id_type=MESH)

    own = [
        pltpu.make_async_copy(
            source.at[:, columns(me * HEAD, HEAD)],
            landing.at[pl.ds(pl.multiple_of(REACH * shard + me * tokens, tokens), tokens), pl.ds(0, HEAD)],
            local.at[number])
        for number, (source, landing) in enumerate(((key, kx), (value, vx)))
    ] + [
        pltpu.make_async_copy(source.at[:, columns(me * group, group)], landing.at[mine, :], local.at[2 + number])
        for number, (source, landing) in enumerate(((query, qb), (cotangent, db)))
    ]
    for which in range(2):
        for step in others:
            kv_copy(which, step).start()
    for copy in own:
        copy.start()

    def start_in(which):
        def body(chunk, carry):
            for step in others:
                in_copy(which, chunk, step).start()
            return carry
        lax.fori_loop(0, chunks, body, 0)

    start_in(0)
    start_in(1)

    documents = lens.shape[0]
    lower = lax.broadcasted_iota(jnp.int32, (documents, HEAD), 0)
    upper = lax.broadcasted_iota(jnp.int32, (documents, HEAD), 1)
    counts = jnp.broadcast_to(lens[...], (documents, HEAD)).astype(F32)
    ends = jnp.sum(jnp.where(lower <= upper, counts, 0.0), axis=0, keepdims=True)
    starts = jnp.sum(jnp.where(lower < upper, counts, 0.0), axis=0, keepdims=True)
    number = lax.broadcasted_iota(jnp.int32, (1, HEAD), 1)
    ends = jnp.where(number == documents, 0.0, ends).astype(jnp.int32)
    starts = jnp.where(number == documents, -1e6, starts).astype(jnp.int32)

    def inside(first, amount):
        at = lax.broadcasted_iota(jnp.int32, (amount, HEAD), 0) + first
        return (at >= starts) & (at < ends)

    qe[...] = jnp.where(inside(place * shard, shard), 0.0, OUTSIDE).astype(BF16)
    kx[:, HEAD:] = jnp.where(inside((place - REACH) * shard, window), 1.0, 0.0).astype(BF16)
    vx[:, HEAD:] = jnp.ones((window, HEAD), BF16)

    for which in range(2):
        own[which].wait()
        for step in others:
            kv_copy(which, step).wait_recv()
        for step in range(1, REACH + 1):
            window_copy(which, step).start()
    own[2].wait()
    for step in range(1, REACH + 1):
        window_copy(0, step).wait_recv()

    def wait_in(which, chunk):
        for step in others:
            in_copy(which, chunk, step).wait_recv()

    def stacked(ref, chunk, pair):
        block = ref[pair * TILE:(pair + 1) * TILE, columns(chunk * wide, wide)]
        return jnp.concatenate([block[:, head * HEAD:(head + 1) * HEAD] for head in range(CHUNK_HEADS)], axis=0)

    def unstacked(block):
        return jnp.concatenate([block[head * TILE:(head + 1) * TILE] for head in range(CHUNK_HEADS)], axis=1)

    def chunk_rows(chunk):
        return pl.ds(pl.multiple_of(chunk * rows, rows), rows)

    scores = (s0, s1)
    at_row = lax.broadcasted_iota(jnp.int32, (rows, TILE), 0) % TILE
    at_column = lax.broadcasted_iota(jnp.int32, (rows, TILE), 1)
    lane = lax.broadcasted_iota(jnp.int32, (rows, HEAD), 1)

    def forward(later, now):
        if later is not None:
            chunk, pair = later
            extra = qe[pair * TILE:(pair + 1) * TILE, :]
            qx = jnp.concatenate([stacked(qb, chunk, pair), jnp.concatenate([extra] * CHUNK_HEADS, axis=0)], axis=1)
        if now is not None:
            chunk_now, pair_now = now
            at = chunk_rows(chunk_now)
            top = s1 if pair_now else s0
            highest = top[:, TILES * TILE:]
        running = None
        for tile in range(TILES):
            span = slice(tile * TILE, (tile + 1) * TILE)
            if later is not None:
                s = dot(qx, kx[pair * TILE + tile * TILE:pair * TILE + (tile + 1) * TILE, :], NT)
                if tile == TILES - 1:
                    s = jnp.where(at_column <= at_row, s, OUTSIDE)
                scores[pair][:, span] = s
                half = jnp.maximum(s[:, :HEAD], s[:, HEAD:])
                running = half if running is None else jnp.maximum(running, half)
            if now is not None:
                shifted = scores[pair_now][:, span] * to_log2 - jnp.concatenate([highest, highest], axis=1)
                pb[tile, pair_now, at, :] = jnp.exp2(shifted).astype(BF16)
        if later is not None:
            most = jnp.max(running, axis=1, keepdims=True) * to_log2
            scores[pair][:, TILES * TILE:] = jnp.broadcast_to(most, (rows, HEAD))
        if now is not None:
            total = None
            for tile in range(TILES):
                first = pair_now * TILE + tile * TILE
                part = dot(pb[tile, pair_now, at, :], vx[first:first + TILE, :], NN)
                total = part if total is None else total + part
            reciprocal = 1.0 / total[:, HEAD:]
            out = total[:, :HEAD] * reciprocal
            inv[pair_now, at, :] = reciprocal
            acc[pair_now, at, :] = out
            ob[pair_now * TILE:(pair_now + 1) * TILE, columns(chunk_now * wide, wide)] = unstacked(out.astype(BF16))

    def send_out(which, chunk):
        for step in others:
            out_copy(which, chunk, step).start()

    wait_in(0, 0)
    forward((0, 0), None)
    for step in range(1, REACH + 1):
        window_copy(1, step).wait_recv()

    def forward_step(chunk, carry):
        forward((chunk, 1), (chunk, 0))
        wait_in(0, chunk + 1)
        forward((chunk + 1, 0), (chunk, 1))
        send_out(0, chunk)
        return carry

    lax.fori_loop(0, chunks - 1, forward_step, 0)
    forward((chunks - 1, 1), (chunks - 1, 0))
    forward(None, (chunks - 1, 1))
    send_out(0, chunks - 1)
    own_out = pltpu.make_async_copy(ob.at[mine, :], attended.at[:, columns(me * group, group)], local.at[4])
    own_out.start()

    own[3].wait()

    def prepare(chunk, carry):
        wait_in(1, chunk)
        at = chunk_rows(chunk)
        for pair in range(pairs):
            given = stacked(db, chunk, pair)
            wide_given = given.astype(F32)
            out = acc[pair, at, :]
            reciprocal = inv[pair, at, :]
            delta = -jnp.sum(wide_given * out, axis=1, keepdims=True)
            high = delta.astype(BF16).astype(F32)
            rest = delta - high
            middle = rest.astype(BF16).astype(F32)
            low = rest - middle
            extra = jnp.where(lane == 0, high, jnp.where(lane == 1, middle, jnp.where(lane == 2, low, 0.0)))
            dox[pair, at, :HEAD] = given
            dox[pair, at, HEAD:] = extra.astype(BF16)
            don[pair, at, :] = (wide_given * reciprocal).astype(BF16)
            qn[pair, at, :] = (stacked(qb, chunk, pair).astype(F32) * (reciprocal * scale)).astype(BF16)
            acc[pair, at, :] = jnp.zeros((rows, HEAD), F32)
        return carry

    lax.fori_loop(0, chunks, prepare, 0)

    def tile_rows(tile):
        return pl.ds(pl.multiple_of(tile * TILE, TILE), TILE)

    def one_chunk(tile, pair, at):
        weights = pb[tile - pair, pair, at, :]
        dweight = dot(dox[pair, at, :], vx[tile_rows(tile), :], NT)
        ds = (weights.astype(F32) * dweight).astype(BF16)
        dsb[pair, at, :] = ds
        acc[pair, at, :] += dot(ds, kx[tile_rows(tile), pl.ds(0, HEAD)], NN)

    def whole_tile(tile, which):
        dk = dv = None
        for pair in which:
            for chunk in range(chunks):
                one_chunk(tile, pair, slice(chunk * rows, (chunk + 1) * rows))
        for pair in which:
            more_k = dot(dsb[pair], qn[pair], TN)
            more_v = dot(pb[tile - pair, pair], don[pair], TN)
            dk = more_k if dk is None else dk + more_k
            dv = more_v if dv is None else dv + more_v
        return dk, dv

    far = shard // TILE

    def store_part(tile, gradients):
        block = tile // far
        at = pl.ds(pl.multiple_of((tile % far) * TILE, TILE), TILE)
        sendb[block, at, :HEAD] = gradients[0].astype(BF16)
        sendb[block, at, HEAD:] = gradients[1].astype(BF16)

    store_part(0, whole_tile(0, (0,)))
    store_part(1, whole_tile(1, (0, 1)))
    part_copy(0).start()

    def backward_step(block, carry):
        store_part(block * far, whole_tile(block * far, (0, 1)))
        store_part(block * far + 1, whole_tile(block * far + 1, (0, 1)))
        part_copy(block).start()
        return carry

    lax.fori_loop(1, REACH, backward_step, 0)

    akk[...] = jnp.zeros_like(akk)
    avv[...] = jnp.zeros_like(avv)
    last = REACH * far

    def last_step(chunk, carry):
        at = chunk_rows(chunk)
        for tile, pair in ((last, 0), (last, 1), (last + 1, 1)):
            one_chunk(tile, pair, at)
            span = slice((tile - last) * TILE, (tile - last + 1) * TILE)
            akk[span, :] += dot(dsb[pair, at, :], qn[pair, at, :], TN)
            avv[span, :] += dot(pb[tile - pair, pair, at, :], don[pair, at, :], TN)
        for pair in range(pairs):
            gradient = acc[pair, at, :] * (inv[pair, at, :] * scale)
            dqb[pair * TILE:(pair + 1) * TILE, columns(chunk * wide, wide)] = unstacked(gradient.astype(BF16))
        send_out(1, chunk)
        return carry

    lax.fori_loop(0, chunks, last_step, 0)
    own_dq = pltpu.make_async_copy(dqb.at[mine, :], grad_query.at[:, columns(me * group, group)], local.at[5])
    own_dq.start()

    for block in range(REACH):
        part_copy(block).wait_recv()
    for which, total in enumerate((akk, avv)):
        span = slice(which * HEAD, (which + 1) * HEAD)
        whole = total[...]
        for block in range(REACH):
            whole = whole + recvb[block, :, span].astype(F32)
        gb[which] = whole.astype(BF16)
    own_g = [
        pltpu.make_async_copy(gb.at[which, mine, :], ref.at[:, columns(me * HEAD, HEAD)], local.at[6 + which])
        for which, ref in enumerate((grad_key, grad_value))
    ]
    for which in range(2):
        for step in others:
            grad_copy(which, step).start()
        own_g[which].start()

    for which in range(2):
        for step in others:
            kv_copy(which, step).wait_send()
        for step in range(1, REACH + 1):
            window_copy(which, step).wait_send()
    for block in range(REACH):
        part_copy(block).wait_send()

    def drain(chunk, carry):
        for step in others:
            in_copy(0, chunk, step).wait_send()
            in_copy(1, chunk, step).wait_send()
            out_copy(0, chunk, step).wait()
            out_copy(1, chunk, step).wait()
        return carry

    lax.fori_loop(0, chunks, drain, 0)
    own_out.wait()
    own_dq.wait()
    for which in range(2):
        own_g[which].wait()
        for step in others:
            grad_copy(which, step).wait()


def per_device(query, key, value, cotangent, lengths):
    cp_size = lax.axis_size("cp")
    hp_size = lax.axis_size("hp")
    tokens = query.shape[0]
    heads = query.shape[1] // (HEAD * hp_size)
    shard = tokens * hp_size
    pairs = shard // TILE
    window = (REACH + 1) * shard
    chunks = heads // CHUNK_HEADS
    rows = TILE * CHUNK_HEADS
    total = heads * TILE
    anywhere = pl.BlockSpec(memory_space=pl.ANY)
    vmem = pltpu.VMEM
    dma = pltpu.SemaphoreType.DMA
    peers = hp_size - 1
    scratch = [
        vmem((shard, heads * HEAD), BF16),
        vmem((shard, heads * HEAD), BF16),
        vmem((window, 2 * HEAD), BF16),
        vmem((window, 2 * HEAD), BF16),
        vmem((shard, HEAD), BF16),
        vmem((rows, TILES * TILE + HEAD), F32),
        vmem((rows, TILES * TILE + HEAD), F32),
        vmem((TILES, pairs, total, TILE), BF16),
        vmem((pairs, total, TILE), BF16),
        vmem((shard, heads * HEAD), BF16),
        vmem((shard, heads * HEAD), BF16),
        vmem((pairs, total, HEAD), F32),
        vmem((pairs, total, HEAD), F32),
        vmem((pairs, total, 2 * HEAD), BF16),
        vmem((pairs, total, HEAD), BF16),
        vmem((pairs, total, HEAD), BF16),
        vmem((shard, HEAD), F32),
        vmem((shard, HEAD), F32),
        vmem((REACH, shard, 2 * HEAD), BF16),
        vmem((REACH, shard, 2 * HEAD), BF16),
        vmem((2, shard, HEAD), BF16),
        dma((2, peers)), dma((2, peers)),
        dma((2, REACH)), dma((2, REACH)),
        dma((chunks, peers)), dma((chunks, peers)),
        dma((chunks, peers)), dma((chunks, peers)),
        dma((chunks, peers)), dma((chunks, peers)),
        dma((chunks, peers)), dma((chunks, peers)),
        dma((REACH,)), dma((REACH,)),
        dma((2, peers)), dma((2, peers)),
        dma((8,)),
    ]
    shape = jax.ShapeDtypeStruct
    return pl.pallas_call(
        functools.partial(kernel, cp_size, hp_size, tokens, heads),
        out_shape=(
            shape(query.shape, BF16),
            shape(query.shape, BF16),
            shape(key.shape, BF16),
            shape(value.shape, BF16),
        ),
        in_specs=[anywhere] * 4 + [pl.BlockSpec(memory_space=pltpu.VMEM)],
        out_specs=[anywhere] * 4,
        scratch_shapes=scratch,
        compiler_params=pltpu.CompilerParams(
            collective_id=0, has_side_effects=True, vmem_limit_bytes=56 << 20
        ),
    )(query, key, value, cotangent, lengths.reshape(-1, 1))


def solution(mesh):
    spec = P(("cp", "hp"), None)
    return jax.shard_map(
        per_device,
        mesh=mesh,
        in_specs=(spec, spec, spec, spec, P()),
        out_specs=(spec, spec, spec, spec),
        check_vma=False,
    )
```

profile of v0, /device:TPU:1, one launch (start us, length us, event | category | flops | bytes accessed | tf_op | source)
XLA Modules:
  0.0 83.9 jit_solution(7850663465475378027)
XLA Ops:
  0.6 0.0 copy-start.3
  0.6 0.6 copy-done.3
  1.3 0.7 copy.9.lens
  2.0 76.9 %shard_map.84 = (bf16[128,4096]{1,0:T(8,128)(2,1)}, bf16[128,4096]{1,0:T(8,128)(2,1)}, bf16[128,512]{1,0:T(8,128)(2,1)}, bf16[128,512]{1,0:T(8,128)(2,1)}) custom-call(bf16[128,4096]{1,0:T(8,128)(2,1)} %query.1, bf16[128,512]{1,0:T(8,128)(2,1)} %key.1, bf16[128,512]{1,0:T(8,128)(2,1)} %value.1, bf16[128,4096]{1,0:T(8,128)(2,1)} %cotangent.1, s32[64,1]{1,0:T(8,128)} %copy.9.lens), custom_call_target="tpu_custom_call" | custom-call | tf_op jit(solution)/shard_map/pallas_call | solution.py:429
  78.9 0.0 copy-start
  78.9 2.4 %copy.14 = bf16[128,4096]{1,0:T(8,128)(2,1)} copy(bf16[128,4096]{1,0:T(8,128)(2,1)} %get-tuple-element.8) | data formatting | bytes 2097152
  81.3 0.0 copy-done
  81.3 0.0 copy-start.2
  81.3 1.0 %copy.15 = bf16[128,4096]{1,0:T(8,128)(2,1)} copy(bf16[128,4096]{1,0:T(8,128)(2,1)S(1)} %copy-done) | data formatting | bytes 2097152
  82.3 0.1 copy-done.2
  82.3 0.0 copy-start.1
  82.3 0.7 copy.16
  83.0 0.3 copy-done.1
  83.3 0.7 copy.17
Async XLA Ops:
  0.6 0.7 copy-start.3
  78.9 2.4 %copy-start = (bf16[128,4096]{1,0:T(8,128)(2,1)S(1)}, bf16[128,4096]{1,0:T(8,128)(2,1)}, u32[]{:S(2)}) copy-start(bf16[128,4096]{1,0:T(8,128)(2,1)} %get-tuple-element.9) | copy-start | bytes 3145732
  81.3 1.0 %copy-start.2 = (bf16[128,512]{1,0:T(8,128)(2,1)S(1)}, bf16[128,512]{1,0:T(8,128)(2,1)}, u32[]{:S(2)}) copy-start(bf16[128,512]{1,0:T(8,128)(2,1)} %get-tuple-element.10) | copy-start | bytes 393220
  82.3 1.0 %copy-start.1 = (bf16[128,512]{1,0:T(8,128)(2,1)S(1)}, bf16[128,512]{1,0:T(8,128)(2,1)}, u32[]{:S(2)}) copy-start(bf16[128,512]{1,0:T(8,128)(2,1)} %get-tuple-element.11) | copy-start | bytes 393220
where the time goes:
time: 84.2 us; the launch traced here: 83.9 us
  Pallas kernels  76.9 us (91%)
  local copies, waits for them, and re-layouts  6.36 us (8%)
    pallas_call x1, Pallas kernels, per_device(): pl.pallas_call(functools.partial(kernel, cp_size, hp_size, tokens, heads)...  76.9 us
    unnamed x12, local copies, waits for them, and re-layouts  5.65 us

commit v1 on v0

--- a/solution.py
+++ b/solution.py
@@ -14,8 +14,8 @@
 TILES = 7
 CHUNK_HEADS = 2
 OUTSIDE = -16384.0
+AT_ONCE = 4
 NT = (((1,), (1,)), ((), ()))
-TN = (((0,), (0,)), ((), ()))
 NN = (((1,), (0,)), ((), ()))
 F32 = jnp.float32
 BF16 = jnp.bfloat16
@@ -28,9 +28,9 @@
 
 def kernel(
     cp_size, hp_size, tokens, heads,
-    query, key, value, cotangent, lens,
+    query, key, value, cotangent, lengths,
     attended, grad_query, grad_key, grad_value,
-    qb, db, kx, vx, qe, s0, s1, pb, dsb, ob, dqb, acc, inv, dox, qn, don, akk, avv, sendb, recvb, gb,
+    lens, qb, db, kx, vx, qe, pb, dsb, ob, dqb, acc, total, top, tops, dox, dt, qt, akk, avv, sendb, recvb, gb,
     kv_send, kv_recv, win_send, win_recv, q_send, q_recv, d_send, d_recv,
     o_send, o_recv, dq_send, dq_recv, part_send, part_recv, g_send, g_recv, local,
 ):
@@ -114,6 +114,7 @@
             send_sem=g_send.at[which, step - 1], recv_sem=g_recv.at[which, step - 1],
             device_id=(place, to), device_id_type=MESH)
 
+    own_lens = pltpu.make_async_copy(lengths, lens, local.at[8])
     own = [
         pltpu.make_async_copy(
             source.at[:, columns(me * HEAD, HEAD)],
@@ -127,6 +128,7 @@
     for which in range(2):
         for step in others:
             kv_copy(which, step).start()
+    own_lens.start()
     for copy in own:
         copy.start()
 
@@ -140,15 +142,21 @@
     start_in(0)
     start_in(1)
 
-    documents = lens.shape[0]
+    documents = lens.shape[1]
     lower = lax.broadcasted_iota(jnp.int32, (documents, HEAD), 0)
     upper = lax.broadcasted_iota(jnp.int32, (documents, HEAD), 1)
-    counts = jnp.broadcast_to(lens[...], (documents, HEAD)).astype(F32)
-    ends = jnp.sum(jnp.where(lower <= upper, counts, 0.0), axis=0, keepdims=True)
-    starts = jnp.sum(jnp.where(lower < upper, counts, 0.0), axis=0, keepdims=True)
+    own_lens.wait()
+    counts = jnp.broadcast_to(lens[...], (8, documents))
+    coarse = (counts // 256).astype(BF16)
+    fine = (counts % 256).astype(BF16)
+
+    def added(mask):
+        taken = jnp.where(mask, 1.0, 0.0).astype(BF16)
+        return (256.0 * dot(coarse, taken, NN) + dot(fine, taken, NN))[:1]
+
     number = lax.broadcasted_iota(jnp.int32, (1, HEAD), 1)
-    ends = jnp.where(number == documents, 0.0, ends).astype(jnp.int32)
-    starts = jnp.where(number == documents, -1e6, starts).astype(jnp.int32)
+    ends = jnp.where(number == documents, 0.0, added(lower <= upper)).astype(jnp.int32)
+    starts = jnp.where(number == documents, -1e6, added(lower < upper)).astype(jnp.int32)
 
     def inside(first, amount):
         at = lax.broadcasted_iota(jnp.int32, (amount, HEAD), 0) + first
@@ -162,11 +170,11 @@
         own[which].wait()
         for step in others:
             kv_copy(which, step).wait_recv()
-        for step in range(1, REACH + 1):
+        window_copy(which, 1).start()
+    for step in range(2, REACH + 1):
+        for which in range(2):
             window_copy(which, step).start()
     own[2].wait()
-    for step in range(1, REACH + 1):
-        window_copy(0, step).wait_recv()
 
     def wait_in(which, chunk):
         for step in others:
@@ -182,69 +190,93 @@
     def chunk_rows(chunk):
         return pl.ds(pl.multiple_of(chunk * rows, rows), rows)
 
-    scores = (s0, s1)
+    far = shard // TILE
+    last = REACH * far
     at_row = lax.broadcasted_iota(jnp.int32, (rows, TILE), 0) % TILE
     at_column = lax.broadcasted_iota(jnp.int32, (rows, TILE), 1)
     lane = lax.broadcasted_iota(jnp.int32, (rows, HEAD), 1)
 
-    def forward(later, now):
-        if later is not None:
-            chunk, pair = later
-            extra = qe[pair * TILE:(pair + 1) * TILE, :]
-            qx = jnp.concatenate([stacked(qb, chunk, pair), jnp.concatenate([extra] * CHUNK_HEADS, axis=0)], axis=1)
-        if now is not None:
-            chunk_now, pair_now = now
-            at = chunk_rows(chunk_now)
-            top = s1 if pair_now else s0
-            highest = top[:, TILES * TILE:]
+    def twice(block):
+        return jnp.concatenate([block, block], axis=1)
+
+    def tiles_of(step, pair):
+        first = (REACH - step) * far
+        return [tile for tile in range(first, first + far) if pair <= tile < pair + TILES]
+
+    def look(step, chunk, pair):
+        extra = qe[pair * TILE:(pair + 1) * TILE, :]
+        qx = jnp.concatenate([stacked(qb, chunk, pair), jnp.concatenate([extra] * CHUNK_HEADS, axis=0)], axis=1)
         running = None
-        for tile in range(TILES):
-            span = slice(tile * TILE, (tile + 1) * TILE)
-            if later is not None:
-                s = dot(qx, kx[pair * TILE + tile * TILE:pair * TILE + (tile + 1) * TILE, :], NT)
-                if tile == TILES - 1:
-                    s = jnp.where(at_column <= at_row, s, OUTSIDE)
-                scores[pair][:, span] = s
-                half = jnp.maximum(s[:, :HEAD], s[:, HEAD:])
-                running = half if running is None else jnp.maximum(running, half)
-            if now is not None:
-                shifted = scores[pair_now][:, span] * to_log2 - jnp.concatenate([highest, highest], axis=1)
-                pb[tile, pair_now, at, :] = jnp.exp2(shifted).astype(BF16)
-        if later is not None:
-            most = jnp.max(running, axis=1, keepdims=True) * to_log2
-            scores[pair][:, TILES * TILE:] = jnp.broadcast_to(most, (rows, HEAD))
-        if now is not None:
-            total = None
-            for tile in range(TILES):
-                first = pair_now * TILE + tile * TILE
-                part = dot(pb[tile, pair_now, at, :], vx[first:first + TILE, :], NN)
-                total = part if total is None else total + part
-            reciprocal = 1.0 / total[:, HEAD:]
-            out = total[:, :HEAD] * reciprocal
-            inv[pair_now, at, :] = reciprocal
-            acc[pair_now, at, :] = out
-            ob[pair_now * TILE:(pair_now + 1) * TILE, columns(chunk_now * wide, wide)] = unstacked(out.astype(BF16))
+        found = []
+        for tile in tiles_of(step, pair):
+            s = dot(qx, kx[tile * TILE:(tile + 1) * TILE, :], NT) * to_log2
+            if tile == last + pair:
+                s = jnp.where(at_column <= at_row, s, OUTSIDE)
+            found.append(s)
+            half = jnp.maximum(s[:, :HEAD], s[:, HEAD:])
+            running = half if running is None else jnp.maximum(running, half)
+        return found, running
+
+    def attend(step, chunk, pair, found, running):
+        at = chunk_rows(chunk)
+        most = jnp.broadcast_to(jnp.max(running, axis=1, keepdims=True), (rows, HEAD))
+        tops[step, pair, at, :] = most
+        part = None
+        for tile, s in zip(tiles_of(step, pair), found):
+            weights = jnp.exp2(s - twice(most)).astype(BF16)
+            pb[tile - pair, pair, at, :] = weights
+            more = dot(weights, vx[tile * TILE:(tile + 1) * TILE, :], NN)
+            part = more if part is None else part + more
+        if step == 0:
+            acc[pair, at, :] = part[:, :HEAD]
+            total[pair, at, :] = part[:, HEAD:]
+            top[pair, at, :] = most
+        else:
+            before = top[pair, at, :]
+            highest = jnp.maximum(before, most)
+            old = jnp.exp2(before - highest)
+            new = jnp.exp2(most - highest)
+            out = acc[pair, at, :] * old + part[:, :HEAD] * new
+            weight = total[pair, at, :] * old + part[:, HEAD:] * new
+            if step < REACH:
+                acc[pair, at, :] = out
+                total[pair, at, :] = weight
+                top[pair, at, :] = highest
+            else:
+                out = out / weight
+                acc[pair, at, :] = out
+                top[pair, at, :] = highest + jnp.log2(weight)
+                ob[pair * TILE:(pair + 1) * TILE, columns(chunk * wide, wide)] = unstacked(out.astype(BF16))
+
+    def forward(step, chunk):
+        work = [(chunk + more, pair) for more in range(AT_ONCE) for pair in range(pairs)]
+        ahead = [look(step, *work[0])]
+        for number, piece in enumerate(work):
+            if number + 1 < len(work):
+                ahead.append(look(step, *work[number + 1]))
+            attend(step, *piece, *ahead[number])
 
     def send_out(which, chunk):
         for step in others:
             out_copy(which, chunk, step).start()
 
-    wait_in(0, 0)
-    forward((0, 0), None)
-    for step in range(1, REACH + 1):
-        window_copy(1, step).wait_recv()
-
-    def forward_step(chunk, carry):
-        forward((chunk, 1), (chunk, 0))
-        wait_in(0, chunk + 1)
-        forward((chunk + 1, 0), (chunk, 1))
-        send_out(0, chunk)
-        return carry
-
-    lax.fori_loop(0, chunks - 1, forward_step, 0)
-    forward((chunks - 1, 1), (chunks - 1, 0))
-    forward(None, (chunks - 1, 1))
-    send_out(0, chunks - 1)
+    for step in range(REACH + 1):
+        if step:
+            window_copy(0, step).wait_recv()
+            window_copy(1, step).wait_recv()
+
+        def forward_step(number, carry, step=step):
+            chunk = number * AT_ONCE
+            for more in range(AT_ONCE):
+                if step == 0:
+                    wait_in(0, chunk + more)
+            forward(step, chunk)
+            for more in range(AT_ONCE):
+                if step == REACH:
+                    send_out(0, chunk + more)
+            return carry
+
+        lax.fori_loop(0, chunks // AT_ONCE, forward_step, 0)
     own_out = pltpu.make_async_copy(ob.at[mine, :], attended.at[:, columns(me * group, group)], local.at[4])
     own_out.start()
 
@@ -257,7 +289,6 @@
             given = stacked(db, chunk, pair)
             wide_given = given.astype(F32)
             out = acc[pair, at, :]
-            reciprocal = inv[pair, at, :]
             delta = -jnp.sum(wide_given * out, axis=1, keepdims=True)
             high = delta.astype(BF16).astype(F32)
             rest = delta - high
@@ -266,8 +297,8 @@
             extra = jnp.where(lane == 0, high, jnp.where(lane == 1, middle, jnp.where(lane == 2, low, 0.0)))
             dox[pair, at, :HEAD] = given
             dox[pair, at, HEAD:] = extra.astype(BF16)
-            don[pair, at, :] = (wide_given * reciprocal).astype(BF16)
-            qn[pair, at, :] = (stacked(qb, chunk, pair).astype(F32) * (reciprocal * scale)).astype(BF16)
+            dt[pair, :, at] = wide_given.T.astype(BF16)
+            qt[pair, :, at] = stacked(qb, chunk, pair).astype(F32).T.astype(BF16)
             acc[pair, at, :] = jnp.zeros((rows, HEAD), F32)
         return carry
 
@@ -277,9 +308,11 @@
         return pl.ds(pl.multiple_of(tile * TILE, TILE), TILE)
 
     def one_chunk(tile, pair, at):
-        weights = pb[tile - pair, pair, at, :]
+        factor = jnp.exp2(tops[REACH - tile // far, pair, at, :] - top[pair, at, :])
+        weights = pb[tile - pair, pair, at, :].astype(F32) * twice(factor)
+        pb[tile - pair, pair, at, :] = weights.astype(BF16)
         dweight = dot(dox[pair, at, :], vx[tile_rows(tile), :], NT)
-        ds = (weights.astype(F32) * dweight).astype(BF16)
+        ds = (weights * dweight).astype(BF16)
         dsb[pair, at, :] = ds
         acc[pair, at, :] += dot(ds, kx[tile_rows(tile), pl.ds(0, HEAD)], NN)
 
@@ -289,19 +322,17 @@
             for chunk in range(chunks):
                 one_chunk(tile, pair, slice(chunk * rows, (chunk + 1) * rows))
         for pair in which:
-            more_k = dot(dsb[pair], qn[pair], TN)
-            more_v = dot(pb[tile - pair, pair], don[pair], TN)
+            more_k = dot(qt[pair], dsb[pair], NN)
+            more_v = dot(dt[pair], pb[tile - pair, pair], NN)
             dk = more_k if dk is None else dk + more_k
             dv = more_v if dv is None else dv + more_v
         return dk, dv
 
-    far = shard // TILE
-
     def store_part(tile, gradients):
         block = tile // far
         at = pl.ds(pl.multiple_of((tile % far) * TILE, TILE), TILE)
-        sendb[block, at, :HEAD] = gradients[0].astype(BF16)
-        sendb[block, at, HEAD:] = gradients[1].astype(BF16)
+        sendb[block, at, :HEAD] = (gradients[0] * scale).T.astype(BF16)
+        sendb[block, at, HEAD:] = gradients[1].T.astype(BF16)
 
     store_part(0, whole_tile(0, (0,)))
     store_part(1, whole_tile(1, (0, 1)))
@@ -317,17 +348,15 @@
 
     akk[...] = jnp.zeros_like(akk)
     avv[...] = jnp.zeros_like(avv)
-    last = REACH * far
-
     def last_step(chunk, carry):
         at = chunk_rows(chunk)
         for tile, pair in ((last, 0), (last, 1), (last + 1, 1)):
             one_chunk(tile, pair, at)
             span = slice((tile - last) * TILE, (tile - last + 1) * TILE)
-            akk[span, :] += dot(dsb[pair, at, :], qn[pair, at, :], TN)
-            avv[span, :] += dot(pb[tile - pair, pair, at, :], don[pair, at, :], TN)
+            akk[:, span] += dot(qt[pair, :, at], dsb[pair, at, :], NN)
+            avv[:, span] += dot(dt[pair, :, at], pb[tile - pair, pair, at, :], NN)
         for pair in range(pairs):
-            gradient = acc[pair, at, :] * (inv[pair, at, :] * scale)
+            gradient = acc[pair, at, :] * scale
             dqb[pair * TILE:(pair + 1) * TILE, columns(chunk * wide, wide)] = unstacked(gradient.astype(BF16))
         send_out(1, chunk)
         return carry
@@ -338,9 +367,9 @@
 
     for block in range(REACH):
         part_copy(block).wait_recv()
-    for which, total in enumerate((akk, avv)):
+    for which, added_up in enumerate((akk, avv)):
         span = slice(which * HEAD, (which + 1) * HEAD)
-        whole = total[...]
+        whole = (added_up[...] if which else added_up[...] * scale).T
         for block in range(REACH):
             whole = whole + recvb[block, :, span].astype(F32)
         gb[which] = whole.astype(BF16)
@@ -393,25 +422,27 @@
     vmem = pltpu.VMEM
     dma = pltpu.SemaphoreType.DMA
     peers = hp_size - 1
+    documents = lengths.shape[0]
     scratch = [
+        vmem((1, documents), jnp.int32),
         vmem((shard, heads * HEAD), BF16),
         vmem((shard, heads * HEAD), BF16),
         vmem((window, 2 * HEAD), BF16),
         vmem((window, 2 * HEAD), BF16),
         vmem((shard, HEAD), BF16),
-        vmem((rows, TILES * TILE + HEAD), F32),
-        vmem((rows, TILES * TILE + HEAD), F32),
         vmem((TILES, pairs, total, TILE), BF16),
         vmem((pairs, total, TILE), BF16),
         vmem((shard, heads * HEAD), BF16),
         vmem((shard, heads * HEAD), BF16),
         vmem((pairs, total, HEAD), F32),
         vmem((pairs, total, HEAD), F32),
+        vmem((pairs, total, HEAD), F32),
+        vmem((REACH + 1, pairs, total, HEAD), F32),
         vmem((pairs, total, 2 * HEAD), BF16),
-        vmem((pairs, total, HEAD), BF16),
-        vmem((pairs, total, HEAD), BF16),
-        vmem((shard, HEAD), F32),
-        vmem((shard, HEAD), F32),
+        vmem((pairs, HEAD, total), BF16),
+        vmem((pairs, HEAD, total), BF16),
+        vmem((HEAD, shard), F32),
+        vmem((HEAD, shard), F32),
         vmem((REACH, shard, 2 * HEAD), BF16),
         vmem((REACH, shard, 2 * HEAD), BF16),
         vmem((2, shard, HEAD), BF16),
@@ -423,24 +454,18 @@
         dma((chunks, peers)), dma((chunks, peers)),
         dma((REACH,)), dma((REACH,)),
         dma((2, peers)), dma((2, peers)),
-        dma((8,)),
+        dma((9,)),
     ]
-    shape = jax.ShapeDtypeStruct
     return pl.pallas_call(
         functools.partial(kernel, cp_size, hp_size, tokens, heads),
-        out_shape=(
-            shape(query.shape, BF16),
-            shape(query.shape, BF16),
-            shape(key.shape, BF16),
-            shape(value.shape, BF16),
-        ),
-        in_specs=[anywhere] * 4 + [pl.BlockSpec(memory_space=pltpu.VMEM)],
-        out_specs=[anywhere] * 4,
+        out_shape=tuple(vmem(array.shape, BF16) for array in (query, query, key, value)),
+        in_specs=[anywhere] * 5,
+        out_specs=[pl.BlockSpec(memory_space=vmem)] * 4,
         scratch_shapes=scratch,
         compiler_params=pltpu.CompilerParams(
             collective_id=0, has_side_effects=True, vmem_limit_bytes=56 << 20
         ),
-    )(query, key, value, cotangent, lengths.reshape(-1, 1))
+    )(query, key, value, cotangent, lengths.reshape(1, -1))
 
 
 def solution(mesh):

time: 84.2 us -> 73.8 us (0.88)
  Pallas kernels: 76.9 us -> 69.8 us
  local copies, waits for them, and re-layouts: 6.36 us -> 3.25 us
    pallas_call x1, Pallas kernels: 76.9 us -> 69.8 us  [per_device(): pl.pallas_call(functools.partial(kernel, cp_size, hp_size, tokens, heads)...]
    unnamed x12 -> x4, local copies, waits for them, and re-layouts: 5.65 us -> 3.25 us
where the time goes in v1:
time: 73.8 us; the launch traced here: 73.7 us
  Pallas kernels  69.8 us (95%)
  local copies, waits for them, and re-layouts  3.25 us (4%)
    pallas_call x1, Pallas kernels, per_device(): pl.pallas_call(functools.partial(kernel, cp_size, hp_size, tokens, heads)...  69.8 us
    unnamed x4, local copies, waits for them, and re-layouts  3.25 us

profile of v1, /device:TPU:1, one launch (start us, length us, event | category | flops | bytes accessed | tf_op | source)
XLA Modules:
  0.0 73.7 jit_solution(3270673145532643910)
XLA Ops:
  0.6 69.8 %shard_map.84 = (bf16[128,4096]{1,0:T(8,128)(2,1)S(1)}, bf16[128,4096]{1,0:T(8,128)(2,1)S(1)}, bf16[128,512]{1,0:T(8,128)(2,1)S(1)}, bf16[128,512]{1,0:T(8,128)(2,1)S(1)}) custom-call(bf16[128,4096]{1,0:T(8,128)(2,1)} %query.1, bf16[128,512]{1,0:T(8,128)(2,1)} %key.1, bf16[128,512]{1,0:T(8,128)(2,1)} %value.1, bf16[128,4096]{1,0:T(8,128)(2,1)} %cotangent.1, ...), custom_call_target="tpu_custom_call" | custom-call | tf_op jit(solution)/shard_map/pallas_call | solution.py:459
  70.5 1.0 %copy.13 = bf16[128,4096]{1,0:T(8,128)(2,1)} copy(bf16[128,4096]{1,0:T(8,128)(2,1)S(1)} %get-tuple-element.4) | data formatting | bytes 2097152
  71.4 0.7 copy.15
  72.1 0.7 copy.16
  72.7 1.0 %copy.14 = bf16[128,4096]{1,0:T(8,128)(2,1)} copy(bf16[128,4096]{1,0:T(8,128)(2,1)S(1)} %get-tuple-element.5) | data formatting | bytes 2097152

commit v2 on v1

--- a/solution.py
+++ b/solution.py
@@ -15,6 +15,7 @@
 CHUNK_HEADS = 2
 OUTSIDE = -16384.0
 AT_ONCE = 4
+SLOTS = 4
 NT = (((1,), (1,)), ((), ()))
 NN = (((1,), (0,)), ((), ()))
 F32 = jnp.float32
@@ -260,7 +261,14 @@
         for step in others:
             out_copy(which, chunk, step).start()
 
+    def turn_queries(chunk, carry):
+        for pair in range(pairs):
+            qt[pair, :, chunk_rows(chunk)] = stacked(qb, chunk, pair).astype(F32).T.astype(BF16)
+        return carry
+
     for step in range(REACH + 1):
+        if step == 1:
+            lax.fori_loop(0, chunks, turn_queries, 0)
         if step:
             window_copy(0, step).wait_recv()
             window_copy(1, step).wait_recv()
@@ -298,63 +306,56 @@
             dox[pair, at, :HEAD] = given
             dox[pair, at, HEAD:] = extra.astype(BF16)
             dt[pair, :, at] = wide_given.T.astype(BF16)
-            qt[pair, :, at] = stacked(qb, chunk, pair).astype(F32).T.astype(BF16)
             acc[pair, at, :] = jnp.zeros((rows, HEAD), F32)
         return carry
 
     lax.fori_loop(0, chunks, prepare, 0)
 
-    def tile_rows(tile):
-        return pl.ds(pl.multiple_of(tile * TILE, TILE), TILE)
-
-    def one_chunk(tile, pair, at):
+    def score_gradient(tile, pair, at):
         factor = jnp.exp2(tops[REACH - tile // far, pair, at, :] - top[pair, at, :])
         weights = pb[tile - pair, pair, at, :].astype(F32) * twice(factor)
         pb[tile - pair, pair, at, :] = weights.astype(BF16)
-        dweight = dot(dox[pair, at, :], vx[tile_rows(tile), :], NT)
+        dweight = dot(dox[pair, at, :], vx[tile * TILE:(tile + 1) * TILE, :], NT)
         ds = (weights * dweight).astype(BF16)
-        dsb[pair, at, :] = ds
-        acc[pair, at, :] += dot(ds, kx[tile_rows(tile), pl.ds(0, HEAD)], NN)
-
-    def whole_tile(tile, which):
+        dsb[tile % SLOTS, pair, at, :] = ds
+        acc[pair, at, :] += dot(ds, kx[tile * TILE:(tile + 1) * TILE, :HEAD], NN)
+
+    def pairs_of(tile):
+        return [pair for pair in range(pairs) if pair <= tile < pair + TILES]
+
+    def query_part(tile):
+        for pair in pairs_of(tile):
+            for chunk in range(chunks):
+                score_gradient(tile, pair, slice(chunk * rows, (chunk + 1) * rows))
+
+    def key_part(tile):
         dk = dv = None
-        for pair in which:
-            for chunk in range(chunks):
-                one_chunk(tile, pair, slice(chunk * rows, (chunk + 1) * rows))
-        for pair in which:
-            more_k = dot(qt[pair], dsb[pair], NN)
+        for pair in pairs_of(tile):
+            more_k = dot(qt[pair], dsb[tile % SLOTS, pair], NN)
             more_v = dot(dt[pair], pb[tile - pair, pair], NN)
             dk = more_k if dk is None else dk + more_k
             dv = more_v if dv is None else dv + more_v
-        return dk, dv
-
-    def store_part(tile, gradients):
-        block = tile // far
-        at = pl.ds(pl.multiple_of((tile % far) * TILE, TILE), TILE)
-        sendb[block, at, :HEAD] = (gradients[0] * scale).T.astype(BF16)
-        sendb[block, at, HEAD:] = gradients[1].T.astype(BF16)
-
-    store_part(0, whole_tile(0, (0,)))
-    store_part(1, whole_tile(1, (0, 1)))
-    part_copy(0).start()
-
-    def backward_step(block, carry):
-        store_part(block * far, whole_tile(block * far, (0, 1)))
-        store_part(block * far + 1, whole_tile(block * far + 1, (0, 1)))
+        return (dk * scale).T, dv.T
+
+    def send_part(block):
+        for tile in range(block * far, (block + 1) * far):
+            at = slice((tile % far) * TILE, (tile % far + 1) * TILE)
+            gradients = key_part(tile)
+            sendb[block, at, :HEAD] = gradients[0].astype(BF16)
+            sendb[block, at, HEAD:] = gradients[1].astype(BF16)
         part_copy(block).start()
-        return carry
-
-    lax.fori_loop(1, REACH, backward_step, 0)
-
-    akk[...] = jnp.zeros_like(akk)
-    avv[...] = jnp.zeros_like(avv)
+
+    for block in range(REACH):
+        for tile in range(block * far, (block + 1) * far):
+            query_part(tile)
+        if block < REACH - 1:
+            send_part(block)
+
     def last_step(chunk, carry):
         at = chunk_rows(chunk)
-        for tile, pair in ((last, 0), (last, 1), (last + 1, 1)):
-            one_chunk(tile, pair, at)
-            span = slice((tile - last) * TILE, (tile - last + 1) * TILE)
-            akk[:, span] += dot(qt[pair, :, at], dsb[pair, at, :], NN)
-            avv[:, span] += dot(dt[pair, :, at], pb[tile - pair, pair, at, :], NN)
+        for tile in range(last, last + far):
+            for pair in pairs_of(tile):
+                score_gradient(tile, pair, at)
         for pair in range(pairs):
             gradient = acc[pair, at, :] * scale
             dqb[pair * TILE:(pair + 1) * TILE, columns(chunk * wide, wide)] = unstacked(gradient.astype(BF16))
@@ -362,6 +363,10 @@
         return carry
 
     lax.fori_loop(0, chunks, last_step, 0)
+    send_part(REACH - 1)
+    for tile in range(last, last + far):
+        span = slice((tile - last) * TILE, (tile - last + 1) * TILE)
+        akk[span, :], avv[span, :] = key_part(tile)
     own_dq = pltpu.make_async_copy(dqb.at[mine, :], grad_query.at[:, columns(me * group, group)], local.at[5])
     own_dq.start()
 
@@ -369,7 +374,7 @@
         part_copy(block).wait_recv()
     for which, added_up in enumerate((akk, avv)):
         span = slice(which * HEAD, (which + 1) * HEAD)
-        whole = (added_up[...] if which else added_up[...] * scale).T
+        whole = added_up[...]
         for block in range(REACH):
             whole = whole + recvb[block, :, span].astype(F32)
         gb[which] = whole.astype(BF16)
@@ -431,7 +436,7 @@
         vmem((window, 2 * HEAD), BF16),
         vmem((shard, HEAD), BF16),
         vmem((TILES, pairs, total, TILE), BF16),
-        vmem((pairs, total, TILE), BF16),
+        vmem((SLOTS, pairs, total, TILE), BF16),
         vmem((shard, heads * HEAD), BF16),
         vmem((shard, heads * HEAD), BF16),
         vmem((pairs, total, HEAD), F32),
@@ -441,8 +446,8 @@
         vmem((pairs, total, 2 * HEAD), BF16),
         vmem((pairs, HEAD, total), BF16),
         vmem((pairs, HEAD, total), BF16),
-        vmem((HEAD, shard), F32),
-        vmem((HEAD, shard), F32),
+        vmem((shard, HEAD), F32),
+        vmem((shard, HEAD), F32),
         vmem((REACH, shard, 2 * HEAD), BF16),
         vmem((REACH, shard, 2 * HEAD), BF16),
         vmem((2, shard, HEAD), BF16),

time: 73.8 us -> 73.2 us (level)
  no operation moved by 1% of the time
where the time goes in v2:
time: 73.2 us; the launch traced here: 73.1 us
  Pallas kernels  69.2 us (95%)
  local copies, waits for them, and re-layouts  3.25 us (4%)
    pallas_call x1, Pallas kernels, per_device(): pl.pallas_call(functools.partial(kernel, cp_size, hp_size, tokens, heads)...  69.2 us
    unnamed x4, local copies, waits for them, and re-layouts  3.25 us

profile of v2, /device:TPU:1, one launch (start us, length us, event | category | flops | bytes accessed | tf_op | source)
XLA Modules:
  0.0 73.1 jit_solution(16999715202227984850)
XLA Ops:
  0.6 69.2 %shard_map.84 = (bf16[128,4096]{1,0:T(8,128)(2,1)S(1)}, bf16[128,4096]{1,0:T(8,128)(2,1)S(1)}, bf16[128,512]{1,0:T(8,128)(2,1)S(1)}, bf16[128,512]{1,0:T(8,128)(2,1)S(1)}) custom-call(bf16[128,4096]{1,0:T(8,128)(2,1)} %query.1, bf16[128,512]{1,0:T(8,128)(2,1)} %key.1, bf16[128,512]{1,0:T(8,128)(2,1)} %value.1, bf16[128,4096]{1,0:T(8,128)(2,1)} %cotangent.1, ...), custom_call_target="tpu_custom_call" | custom-call | tf_op jit(solution)/shard_map/pallas_call | solution.py:464
  69.9 1.0 %copy.13 = bf16[128,4096]{1,0:T(8,128)(2,1)} copy(bf16[128,4096]{1,0:T(8,128)(2,1)S(1)} %get-tuple-element.4) | data formatting | bytes 2097152
  70.8 0.7 copy.15
  71.5 0.7 copy.16
  72.1 1.0 %copy.14 = bf16[128,4096]{1,0:T(8,128)(2,1)} copy(bf16[128,4096]{1,0:T(8,128)(2,1)S(1)} %get-tuple-element.5) | data formatting | bytes 2097152
